TPU v7x, 512 devices: a whole 4x4x16 slice. The times are simulated.
512 devices in a mesh: band: 8 (over y, x_lo), space: 64 (over z, x_hi, core).
Axes of the slice: x: 4 (x_hi: 2, x_lo: 2; x = x_hi * 2 + x_lo), y: 4, z: 16, core: 2. Of those that a mesh axis runs over, the one named last changes fastest.
Arguments:
- orbitals: bfloat16 [256, 512, 16, 128], P('band', 'space'), may hold values from -6 to 6
- filters: float32 [3, 14], replicated, may hold values from -1.5 to 1.5
- panels: bfloat16 [256, 256], P('band'), may hold values from -0.375 to 0.375
Outputs:
- rotated: bfloat16 [256, 512, 16, 128], P('band', 'space')
- kinetic_rows: float32 [256, 256], P('band')
All inputs are finite; a program needn't handle non-finite values.
Results may differ from a plain program's by a relative error of at most 0.0049.
Values may be sent and summed in bfloat16 or wider, within the bound.
A program may use at most 64 MiB of HBM per device.

v0:
```python
import jax
import jax.numpy as jnp
from jax import lax
from jax.sharding import PartitionSpec as P


def extended(x, sides, width):
    for axis, dim in sides:
        devices, length = (lax.axis_size(axis), x.shape[dim])
        up = [(i, (i + 1) % devices) for i in range(devices - 1)]
        down = [(j, i) for i, j in up]
        last = lax.slice_in_dim(x, length - width, length, axis=dim)
        first = lax.slice_in_dim(x, 0, width, axis=dim)
        before = lax.ppermute(last, axis, up)
        after = lax.ppermute(first, axis, down)
        x = jnp.concatenate([before, x, after], axis=dim)
    return x


def local_pass(field, taps, axis):
    count = field.shape[axis]
    widths = [(0, 0)] * field.ndim
    widths[axis] = (7, 6)
    padded = jnp.pad(field, widths)
    total = jnp.zeros(field.shape, jnp.float32)
    for k in range(14):
        total = total + taps[k] * lax.slice_in_dim(padded, k, k + count, axis=axis)
    return total


def on_device(orbitals, filters, panels):
    orb_dev, slab, width_y, width_z = orbitals.shape
    padded = extended(orbitals, (("space", 1),), 7)
    values = padded.astype(jnp.float32)
    along_x = jnp.zeros(orbitals.shape, jnp.float32)
    for k in range(14):
        along_x = along_x + filters[0, k] * lax.slice_in_dim(values, k, k + slab, axis=1)
    inner = lax.slice_in_dim(values, 7, 7 + slab, axis=1)
    image = (along_x + local_pass(inner, filters[1], 2) + local_pass(inner, filters[2], 3)).astype(
        jnp.bfloat16
    )
    scale = 1.0 / (slab * lax.axis_size("space") * width_y * width_z)
    flat_own = orbitals.reshape(orb_dev, -1)
    piece = lax.all_gather(image, "band", axis=0, tiled=True)
    count = piece.shape[0]
    flat = piece.reshape(count, -1)
    rot_sum = jnp.dot(panels, flat, preferred_element_type=jnp.float32)
    block = lax.dot_general(
        flat_own, flat, (((1,), (1,)), ((), ())), preferred_element_type=jnp.float32
    )
    kin_rows = block
    rot_sum, kin_rows = (rot_sum, kin_rows)
    kin_rows = lax.psum(kin_rows * scale, "space")
    return (rot_sum.astype(jnp.bfloat16).reshape(orbitals.shape), kin_rows)


def solution(mesh):
    return jax.shard_map(
        on_device,
        mesh=mesh,
        in_specs=(P("band", "space", None, None), P(), P("band", None)),
        out_specs=(P("band", "space", None, None), P("band", None)),
        check_vma=False,
    )
```

profile of v0, /device:TPU:1, one launch (start us, length us, event | category | flops | bytes accessed | tf_op | source)
XLA Modules:
  0.0 536.4 jit_solution(10993816938917186232)
XLA Ops:
  7.2 0.0 copy-start
  7.2 0.0 all-gather.2.cloned.1.call-start
  7.2 1.9 copy.9
  9.1 0.0 copy-start.3
  9.1 0.4 fusion.72
  9.5 6.0 %collective-permute-start = (bf16[32,7,16,128]{3,0,2,1:T(8,128)(2,1)S(1)}, bf16[32,7,16,128]{3,0,2,1:T(8,128)(2,1)S(1)}, u32[]{:S(2)}, u32[]{:S(2)}) collective-permute-start(bf16[32,7,16,128]{3,0,2,1:T(8,128)(2,1)S(1)} %get-tuple-element.2), channel_id=1, source_target_pairs={{0,1},{1,2},{2,3},{3,4},{4,5},{5,6},{6,7},{7,8},{8,9},{9,10},{10,1... | collective-permute-start | bytes 2752520 | tf_op jit(solution)/shard_map/ppermute | solution.py:14
  15.6 4.1 collective-permute-start.1
  19.7 0.0 copy-done.3
  19.7 0.7 fusion.75
  20.3 0.7 fusion.73
  21.1 0.7 fusion.74
  21.8 13.9 %collective-permute-done = bf16[32,7,16,128]{3,0,2,1:T(8,128)(2,1)S(1)} collective-permute-done((bf16[32,7,16,128]{3,0,2,1:T(8,128)(2,1)S(1)}, bf16[32,7,16,128]{3,0,2,1:T(8,128)(2,1)S(1)}, u32[]{:S(2)}, u32[]{:S(2)}) %collective-permute-start) | collective-permute-done | bytes 917536 | tf_op jit(solution)/shard_map/ppermute | solution.py:14
  35.7 0.0 collective-permute-done.1
  35.7 0.4 maximum_convert_fusion
  36.2 0.2 slice.406
  36.3 34.6 %fusion.67 = bf16[32,8,16,128]{3,0,2,1:T(8,128)(2,1)} fusion(f32[32,8,16,128]{3,0,2,1:T(8,128)S(1)} %slice.406, f32[32,22,16,128]{3,0,2,1:T(8,128)S(1)} %maximum_convert_fusion, f32[]{:T(128)} %bitcast.41, f32[]{:T(128)} %bitcast.40, f32[]{:T(128)} %bitcast.39, f32[]{:T(128)} %bitcast.38, f32[]{:T(128)} %bitcast.37, f32[]{:T(128)} %bitcast.36, f32[]{:T(128)} %bitcast.35, ...), kind=kLoop, calls=%fused_computation.108 | loop fusion | flops 44040192 | bytes 30408872 | tf_op jit(solution)/shard_map/convert_element_type | solution.py:39
  70.9 0.0 all-gather.2.cloned.1.call-update
  70.9 181.3 %all-gather.2.cloned.1.call-done = bf16[256,8,16,128]{3,0,2,1:T(8,128)(2,1)} async-done(((bf16[32,8,16,128]{3,0,2,1:T(8,128)(2,1)}), bf16[256,8,16,128]{3,0,2,1:T(8,128)(2,1)}) %all-gather.2.cloned.1.call-update) | async-done | bytes 8388624 | tf_op jit(solution)/shard_map/all_gather | solution.py:44
  252.3 11.4 %copy.12 = bf16[256,8,16,128]{0,3,2,1:T(8,128)(2,1)} copy(bf16[256,8,16,128]{3,0,2,1:T(8,128)(2,1)} %all-gather.2.cloned.1.call-done) | data formatting | bytes 16777216 | tf_op jit(solution)/shard_map/all_gather | solution.py:44
  263.6 0.0 copy-done
  263.6 0.0 copy-start.1
  263.7 6.1 %fusion.68 = bf16[4,8,128,128]{3,1,2,0:T(8,128)(2,1)S(1)} fusion(bf16[256,16384]{0,1:T(8,128)(2,1)} %bitcast.61, bf16[32,256]{1,0:T(8,128)(2,1)S(1)} %copy-done), kind=kOutput, calls=%fused_computation.109 | convolution fusion | flops 268959744 | bytes 9453568 | tf_op jit(solution)/shard_map/dot_general | solution.py:47
  269.7 0.0 copy-start.2
  269.7 1.2 copy.15
  270.9 0.0 copy-done.1
  270.9 0.2 copy-done.2
  271.1 2.6 fusion.70
  273.7 255.8 %psum.7 = f32[32,256]{1,0:T(8,128)} all-reduce(f32[32,256]{1,0:T(8,128)S(1)} %fusion.70), channel_id=1, replica_groups=mesh['band'=8,'space'=64] {'space'}, use_global_device_ids=true, to_apply=%region_0.1 | all-reduce | flops 8192 | bytes 65536 | tf_op jit(solution)/shard_map/psum | solution.py:53
Async XLA Ops:
  7.2 256.5 %copy-start = (bf16[32,256]{1,0:T(8,128)(2,1)S(1)}, bf16[32,256]{1,0:T(8,128)(2,1)}, u32[]{:S(2)}) copy-start(bf16[32,256]{1,0:T(8,128)(2,1)} %param.5) | copy-start | bytes 49156
  7.2 245.1 %all-gather.2.cloned.1.call-start = ((), (), s32[]{:S(2)}) async-start(), calls=%async_computation | async-start | bytes 9437184 | tf_op jit(solution)/shard_map/all_gather | solution.py:44
  9.1 10.5 %copy-start.3 = (f32[3,14]{1,0:T(4,128)S(1)}, f32[3,14]{1,0:T(4,128)}, u32[]{:S(2)}) copy-start(f32[3,14]{1,0:T(4,128)} %param.4) | copy-start | bytes 508
  9.5 26.2 %collective-permute-start = (bf16[32,7,16,128]{3,0,2,1:T(8,128)(2,1)S(1)}, bf16[32,7,16,128]{3,0,2,1:T(8,128)(2,1)S(1)}, u32[]{:S(2)}, u32[]{:S(2)}) collective-permute-start(bf16[32,7,16,128]{3,0,2,1:T(8,128)(2,1)S(1)} %get-tuple-element.2), channel_id=1, source_target_pairs={{0,1},{1,2},{2,3},{3,4},{4,5},{5,6},{6,7},{7,8},{8,9},{9,10},{10,1... | collective-permute-start | bytes 2752520 | tf_op jit(solution)/shard_map/ppermute | solution.py:14
  15.6 20.2 %collective-permute-start.1 = (bf16[32,7,16,128]{3,0,2,1:T(8,128)(2,1)S(1)}, bf16[32,7,16,128]{3,0,2,1:T(8,128)(2,1)S(1)}, u32[]{:S(2)}, u32[]{:S(2)}) collective-permute-start(bf16[32,7,16,128]{3,0,2,1:T(8,128)(2,1)S(1)} %get-tuple-element.3), channel_id=1, source_target_pairs={{1,0},{2,1},{3,2},{4,3},{5,4},{6,5},{7,6},{8,7},{9,8},{10,9},{11,1... | collective-permute-start | bytes 2752520 | tf_op jit(solution)/shard_map/ppermute | solution.py:15
  263.6 7.3 %copy-start.1 = (bf16[256,8,16,128]{3,0,2,1:T(8,128)(2,1)S(1)}, bf16[256,8,16,128]{3,0,2,1:T(8,128)(2,1)}, u32[]{:S(2)}) copy-start(bf16[256,8,16,128]{3,0,2,1:T(8,128)(2,1)} %all-gather.2.cloned.1.call-done) | copy-start | bytes 25165828
  269.7 1.4 copy-start.2
Sparse Core Ops, SparseCore 0:
  71.0 181.1 all-gather.1
where the time goes:
time: 542 us; the launch traced here: 536 us
  blocking collectives  256 us (47%)
  waiting for transfers between devices  195 us (36%)
  other arithmetic  35 us (6%)
  local copies, waits for them, and re-layouts  17.3 us (3%)
  between operations  14.1 us (3%)
  starting transfers between devices  10.2 us (2%)
  matrix products  8.65 us (2%)
    psum x1, blocking collectives, on_device(): kin_rows = lax.psum(kin_rows * scale, 'space')  256 us
    all_gather x1, waiting for transfers between devices, on_device(): piece = lax.all_gather(image, 'band', axis=0, tiled=True)  181 us
    convert_element_type x1, other arithmetic, on_device(): (along_x + local_pass(inner, filters[1], 2) + local_pass(inner, filters[2...  34.6 us
    ppermute x1, waiting for transfers between devices, extended(): before = lax.ppermute(last, axis, up)  13.9 us
    all_gather x1, local copies, waits for them, and re-layouts, on_device(): piece = lax.all_gather(image, 'band', axis=0, tiled=True)  11.4 us
  transfers between devices with their start and end apart: 3, of which 2 were waited for; matrix products, arithmetic and copies ran while one was open for 0% of the time, Pallas kernels for 0%

commit v1 on v0

v1 whole, which is shorter than its diff:
```python
import functools

import jax
import jax.numpy as jnp
from jax import lax
from jax.experimental import pallas as pl
from jax.experimental.pallas import tpu as pltpu
from jax.sharding import PartitionSpec as P

MESH = pl.DeviceIdType.MESH
F32, BF16 = jnp.float32, jnp.bfloat16
BEFORE, AFTER = 7, 6
NY, NX = 4, 2
NG = 4
ORB, PLANES, ROWS, LANES = 32, 8, 16, 128
CHUNKS = PLANES // NY
ALL = ORB * NY * NX


def band_matrix(taps, row):
    a = lax.broadcasted_iota(jnp.int32, (LANES, LANES), 0)
    b = lax.broadcasted_iota(jnp.int32, (LANES, LANES), 1)
    total = jnp.zeros((LANES, LANES), F32)
    for k in range(14):
        total = jnp.where(a - b == k - BEFORE, taps[row, k], total)
    high = total.astype(BF16)
    low = (total - high.astype(F32)).astype(BF16)
    return jnp.concatenate([high, low], axis=0)


def kernel(
    nz,
    taps, psi, panels,
    out, kin,
    left, right, acc, img, psi_all, img_all, rot, own_panels, kacc, ky, kg, kz, kzs, zmat,
    halo_send, halo_recv, psi_send, psi_recv, pan_send, pan_recv, img_send, img_recv,
    fwd_send, fwd_recv, rot_send, rot_recv, ky_send, ky_recv, kg_send, kg_recv, kz_send, kz_recv, ka_send, ka_recv,
):
    band, space = lax.axis_index("band"), lax.axis_index("space")
    y, xl = band // NX, band % NX
    z, g = space // NG, space % NG
    slabs = nz * NG

    def y_peer(k):
        return lax.rem(y + k, NY)

    def remote(src, dst, send, recv, b, s):
        return pltpu.make_async_remote_copy(
            src_ref=src, dst_ref=dst, send_sem=send, recv_sem=recv, device_id=(b, s), device_id_type=MESH
        )

    partner = y * NX + (1 - xl)

    barrier = pltpu.get_barrier_semaphore()

    def greet(b, s):
        pl.semaphore_signal(barrier, inc=1, device_id=(b, s), device_id_type=MESH)

    for k in range(1, NY):
        greet(y_peer(k) * NX + xl, space)
    greet(partner, space)
    greet(band, lax.rem(space + 1, slabs))
    greet(band, lax.rem(space + slabs - 1, slabs))
    for k in range(1, NG):
        greet(band, z * NG + lax.rem(g + k, NG))

    def greet_z(k, carry):
        greet(band, lax.rem(z + k, nz) * NG + g)
        return carry

    lax.fori_loop(1, nz, greet_z, 0)
    pl.semaphore_wait(barrier, NY - 1 + 1 + 2 + NG - 1 + nz - 1)

    up = remote(psi.at[pl.ds(PLANES - BEFORE, BEFORE)], left, halo_send.at[0], halo_recv.at[0], band, space + 1)
    split = 2
    down = [
        remote(psi.at[pl.ds(0, split)], right.at[pl.ds(0, split)], halo_send.at[1], halo_recv.at[1], band, space - 1),
        remote(
            psi.at[pl.ds(split, AFTER - split)], right.at[pl.ds(split, AFTER - split)],
            halo_send.at[2], halo_recv.at[2], band, space - 1,
        ),
    ]
    first, last = space == 0, space == slabs - 1

    @pl.when(jnp.logical_not(last))
    def _():
        up.start()

    @pl.when(jnp.logical_not(first))
    def _():
        down[0].start()
        down[1].start()

    def psi_copy(k, c):
        to = y_peer(k)
        return remote(
            psi.at[c * NY + to], psi_all.at[c, :, pl.ds(pl.multiple_of(y * ORB, ORB), ORB), :],
            psi_send.at[k, c], psi_recv.at[k, c], to * NX + xl, space,
        )

    def panel_copy(k):
        return remote(
            panels, own_panels.at[pl.ds(pl.multiple_of(y * ORB, ORB), ORB), :],
            pan_send.at[k], pan_recv.at[k], y_peer(k) * NX + xl, space,
        )

    for k in (1, 3, 2):
        panel_copy(k).start()
        for c in range(CHUNKS):
            psi_copy(k, c).start()
    mine = pl.ds(pl.multiple_of(y * ORB, ORB), ORB)
    own_panels[mine, :] = panels[...]
    for c in range(CHUNKS):
        psi_all[c, :, mine, :] = psi[c * NY + y]

    @pl.when(first)
    def _():
        left[...] = jnp.zeros(left.shape, BF16)

    @pl.when(last)
    def _():
        right[...] = jnp.zeros(right.shape, BF16)

    zmat[...] = band_matrix(taps, 2)

    def along_z(p, carry):
        v = psi[p].reshape(ROWS * ORB, LANES)
        r = jnp.dot(jnp.concatenate([v, v], axis=1), zmat[...], preferred_element_type=F32)
        acc[p] = r.reshape(ROWS, ORB, LANES)
        return carry

    lax.fori_loop(0, PLANES, along_z, 0)

    half = 16

    def along_y(i, carry):
        p, h = i // 2, pl.ds(pl.multiple_of((i % 2) * half, half), half)
        v = [psi[p, r, h, :].astype(F32) for r in range(ROWS)]
        for r in range(ROWS):
            total = acc[p, r, h, :]
            for k in range(14):
                if 0 <= r + k - BEFORE < ROWS:
                    total = total + taps[1, k] * v[r + k - BEFORE]
            acc[p, r, h, :] = total
        return carry

    lax.fori_loop(0, PLANES * 2, along_y, 0)

    def along_x(i, carry):
        r, h = i // 2, pl.ds(pl.multiple_of((i % 2) * half, half), half)
        v = [psi[q, r, h, :].astype(F32) for q in range(PLANES)]
        for p in range(PLANES):
            total = acc[p, r, h, :]
            for k in range(14):
                if 0 <= p + k - BEFORE < PLANES:
                    total = total + taps[0, k] * v[p + k - BEFORE]
            acc[p, r, h, :] = total
        return carry

    lax.fori_loop(0, ROWS * 2, along_x, 0)

    def finish(c):
        planes = range(c * NY, (c + 1) * NY)
        lefts = [q for q in range(BEFORE) if any(0 <= q - p < 14 for p in planes)]
        rights = [q for q in range(AFTER) if any(0 <= q + BEFORE + PLANES - p < 14 for p in planes)]

        def body(i, carry):
            r, h = i // 2, pl.ds(pl.multiple_of((i % 2) * half, half), half)
            lv = {q: left[q, r, h, :].astype(F32) for q in lefts}
            rv = {q: right[q, r, h, :].astype(F32) for q in rights}
            for p in planes:
                total = acc[p, r, h, :]
                for q in lefts:
                    k = q - p
                    if 0 <= k < 14:
                        total = total + taps[0, k] * lv[q]
                for q in rights:
                    k = q + BEFORE + PLANES - p
                    if 0 <= k < 14:
                        total = total + taps[0, k] * rv[q]
                img[p, r, h, :] = total.astype(BF16)
            return carry

        lax.fori_loop(0, ROWS * 2, body, 0)

    def slot(b):
        return pl.ds(pl.multiple_of(b * ORB, ORB), ORB)

    def img_copy(k, c):
        to = y_peer(k)
        return remote(
            img.at[c * NY + to], img_all.at[c, :, slot(band), :],
            img_send.at[k, c], img_recv.at[k, c], to * NX + xl, space,
        )

    def fwd_copy(k, c):
        of = lax.rem(y + NY - k, NY) * NX + xl
        src = img.at[c * NY + y] if k == 0 else img_all.at[c, :, slot(of), :]
        return remote(src, img_all.at[c, :, slot(of), :], fwd_send.at[k, c], fwd_recv.at[k, c], partner, space)

    for c in range(CHUNKS):
        if c == 0:

            @pl.when(jnp.logical_not(first))
            def _():
                up.wait_recv()

            @pl.when(jnp.logical_not(last))
            def _():
                down[0].wait_recv()
        else:

            @pl.when(jnp.logical_not(last))
            def _():
                down[1].wait_recv()

        finish(c)
        for k in (2, 1, 3):
            img_copy(k, c).start()
        fwd_copy(0, c).start()
        img_all[c, :, slot(band), :] = img[c * NY + y]

    for k in range(1, NY):
        panel_copy(k).wait_recv()
        for c in range(CHUNKS):
            psi_copy(k, c).wait_recv()

    def rot_copy(k, c):
        to = y_peer(k)
        return remote(
            rot.at[c, :, slot(to), :], out.at[c * NY + y], rot_send.at[k, c], rot_recv.at[k, c], to * NX + xl, space
        )

    kacc[...] = jnp.zeros(kacc.shape, F32)
    for c in range(CHUNKS):
        for k in (1, 3, 2):
            img_copy(k, c).wait_recv()
            fwd_copy(k, c).start()
    for c in range(CHUNKS):
        for k in range(NY):
            fwd_copy(k, c).wait_recv()
        group = 4

        def rotate(i, carry):
            at = i * group
            images = jnp.concatenate([img_all[c, at + j] for j in range(group)], axis=1)
            r = jnp.dot(own_panels[...], images, preferred_element_type=F32).astype(BF16)
            for j in range(group):
                rot[c, at + j] = r[:, j * LANES : (j + 1) * LANES]
            values = jnp.concatenate([psi_all[c, at + j] for j in range(group)], axis=1)
            kacc[...] += lax.dot_general(values, images, (((1,), (1,)), ((), ())), preferred_element_type=F32)
            return carry

        lax.fori_loop(0, ROWS // group, rotate, 0)
        for k in (2, 1, 3):
            rot_copy(k, c).start()
        out[c * NY + y] = rot[c, :, slot(y), :]

    def ky_copy(k):
        to = y_peer(k)
        return remote(kacc.at[slot(to), :], ky.at[k], ky_send.at[k], ky_recv.at[k], to * NX + xl, space)

    for k in range(1, NY):
        ky_copy(k).start()
    for k in range(1, NY):
        ky_copy(k).wait_recv()
    ky[0] = (kacc[slot(y), :] + ky[1]) + (ky[2] + ky[3])
    eight = ORB // NG

    def kg_copy(k):
        to = lax.rem(g + k, NG)
        return remote(
            ky.at[0, pl.ds(pl.multiple_of(to * eight, eight), eight), :], kg.at[k],
            kg_send.at[k], kg_recv.at[k], band, z * NG + to,
        )

    for k in range(1, NG):
        kg_copy(k).start()
    for k in range(1, NG):
        kg_copy(k).wait_recv()
    scale = 1.0 / (slabs * PLANES * ROWS * LANES)
    kzs[...] = ((ky[0, pl.ds(pl.multiple_of(g * eight, eight), eight), :] + kg[1]) + (kg[2] + kg[3])) * scale

    def kz_copy(k):
        return remote(kzs, kz.at[z], kz_send.at[k], kz_recv.at[k], band, lax.rem(z + k, nz) * NG + g)

    def kz_start(k, carry):
        kz_copy(k).start()
        return carry

    def kz_wait(k, carry):
        kz_copy(k).wait_recv()
        return carry

    lax.fori_loop(1, nz, kz_start, 0)
    kz[z] = kzs[...]
    lax.fori_loop(1, nz, kz_wait, 0)
    rows = pl.ds(pl.multiple_of(g * eight, eight), eight)
    total = kz[0]
    for i in range(1, nz):
        total = total + kz[i]
    kin[rows, :] = total

    def ka_copy(k):
        return remote(
            kin.at[rows, :], kin.at[rows, :], ka_send.at[k], ka_recv.at[k], band, z * NG + lax.rem(g + k, NG)
        )

    for k in range(1, NG):
        ka_copy(k).start()
    for k in range(1, NG):
        ka_copy(k).wait_recv()

    for c in range(CHUNKS):
        for k in range(1, NY):
            rot_copy(k, c).wait_recv()

    @pl.when(jnp.logical_not(last))
    def _():
        up.wait_send()

    @pl.when(jnp.logical_not(first))
    def _():
        down[0].wait_send()
        down[1].wait_send()

    for k in range(1, NY):
        panel_copy(k).wait_send()
        ky_copy(k).wait_send()
        for c in range(CHUNKS):
            psi_copy(k, c).wait_send()
            img_copy(k, c).wait_send()
            rot_copy(k, c).wait_send()
    for k in range(NY):
        for c in range(CHUNKS):
            fwd_copy(k, c).wait_send()
    for k in range(1, NG):
        kg_copy(k).wait_send()
        ka_copy(k).wait_send()

    def kz_wait_send(k, carry):
        kz_copy(k).wait_send()
        return carry

    lax.fori_loop(1, nz, kz_wait_send, 0)


def on_device(nz, orbitals, filters, panels):
    psi = jnp.transpose(orbitals, (1, 2, 0, 3))
    vmem = pltpu.VMEM
    dma = pltpu.SemaphoreType.DMA
    eight = ORB // NG
    rotated, kin = pl.pallas_call(
        functools.partial(kernel, nz),
        out_shape=(
            jax.ShapeDtypeStruct((PLANES, ROWS, ORB, LANES), BF16),
            jax.ShapeDtypeStruct((ORB, ALL), F32),
        ),
        in_specs=[
            pl.BlockSpec(memory_space=pltpu.SMEM),
            pl.BlockSpec(memory_space=vmem),
            pl.BlockSpec(memory_space=vmem),
        ],
        out_specs=(pl.BlockSpec(memory_space=vmem), pl.BlockSpec(memory_space=vmem)),
        scratch_shapes=[
            vmem((BEFORE, ROWS, ORB, LANES), BF16),
            vmem((AFTER, ROWS, ORB, LANES), BF16),
            vmem((PLANES, ROWS, ORB, LANES), F32),
            vmem((PLANES, ROWS, ORB, LANES), BF16),
            vmem((CHUNKS, ROWS, ORB * NY, LANES), BF16),
            vmem((CHUNKS, ROWS, ALL, LANES), BF16),
            vmem((CHUNKS, ROWS, ORB * NY, LANES), BF16),
            vmem((ORB * NY, ALL), BF16),
            vmem((ORB * NY, ALL), F32),
            vmem((NY, ORB, ALL), F32),
            vmem((NG, eight, ALL), F32),
            vmem((nz, eight, ALL), F32),
            vmem((eight, ALL), F32),
            vmem((2 * LANES, LANES), BF16),
            dma((3,)), dma((3,)),
            dma((NY, CHUNKS)), dma((NY, CHUNKS)),
            dma((NY,)), dma((NY,)),
            dma((NY, CHUNKS)), dma((NY, CHUNKS)),
            dma((NY, CHUNKS)), dma((NY, CHUNKS)),
            dma((NY, CHUNKS)), dma((NY, CHUNKS)),
            dma((NY,)), dma((NY,)),
            dma((NG,)), dma((NG,)),
            dma((nz,)), dma((nz,)),
            dma((NG,)), dma((NG,)),
        ],
        compiler_params=pltpu.CompilerParams(
            collective_id=0, has_side_effects=True, vmem_limit_bytes=40 * 1024 * 1024
        ),
    )(filters, psi, panels)
    return jnp.transpose(rotated, (2, 0, 1, 3)), kin


def solution(mesh):
    return jax.shard_map(
        functools.partial(on_device, mesh.shape["space"] // NG),
        mesh=mesh,
        in_specs=(P("band", "space", None, None), P(), P("band", None)),
        out_specs=(P("band", "space", None, None), P("band", None)),
        check_vma=False,
    )
```

time: 542 us -> 89.5 us (0.17)
  blocking collectives: 256 us -> 0 us
  waiting for transfers between devices: 195 us -> 0 us
  Pallas kernels: 0 us -> 84.5 us
  other arithmetic: 35 us -> 0 us
  between operations: 14.1 us -> 0.67 us
  local copies, waits for them, and re-layouts: 17.3 us -> 3.92 us
  starting transfers between devices: 10.2 us -> 0 us
  matrix products: 8.65 us -> 0 us
    psum x1 -> x0, blocking collectives: 256 us -> none  [on_device(): kin_rows = lax.psum(kin_rows * scale, 'space')]
    all_gather x1 -> x0, waiting for transfers between devices: 181 us -> none  [on_device(): piece = lax.all_gather(image, 'band', axis=0, tiled=True)]
    pallas_call x0 -> x1, Pallas kernels: none -> 84.5 us  [on_device(): pl.pallas_call(functools.partial(kernel, nz), out_shape=(jax.ShapeDtypeSt...]
    convert_element_type x2 -> x0, other arithmetic: 35 us -> none  [the longest x1 34.6 us: on_device(): (along_x + local_pass(inner, filters[1], 2) + local_pass(inner, filters[2...]
    ppermute x2 -> x0, waiting for transfers between devices: 13.9 us -> none  [the longest x1 13.9 us: extended(): before = lax.ppermute(last, axis, up)]
    all_gather x1 -> x0, local copies, waits for them, and re-layouts: 11.4 us -> none  [on_device(): piece = lax.all_gather(image, 'band', axis=0, tiled=True)]
    ppermute x2 -> x0, starting transfers between devices: 10.1 us -> none  [the longest x1 6.04 us: extended(): before = lax.ppermute(last, axis, up)]
    dot_general x2 -> x0, matrix products: 8.65 us -> none  [the longest x1 6.05 us: on_device(): rot_sum = jnp.dot(panels, flat, preferred_element_type=jnp.float32)]
  transfers between devices with their start and end apart: 3 -> 0, of which waited for: 2 -> 0; matrix products, arithmetic and copies ran while one was open for 0% -> 0% of each run, Pallas kernels for 0% -> 0%
where the time goes in v1:
time: 89.5 us; the launch traced here: 89.1 us
  Pallas kernels  84.5 us (94%)
  local copies, waits for them, and re-layouts  3.92 us (4%)
    pallas_call x1, Pallas kernels, on_device(): pl.pallas_call(functools.partial(kernel, nz), out_shape=(jax.ShapeDtypeSt...  84.5 us
    unnamed x7, local copies, waits for them, and re-layouts  3.92 us

profile of v1, /device:TPU:1, one launch (start us, length us, event | category | flops | bytes accessed | tf_op | source)
XLA Modules:
  0.0 89.1 jit_solution(8962840129038449377)
XLA Ops:
  0.6 0.0 copy-start
  0.6 0.0 copy-start.1
  0.6 1.9 %copy.8 = bf16[32,8,16,128]{3,0,2,1:T(8,128)(2,1)S(1)} copy(bf16[32,8,16,128]{3,2,1,0:T(8,128)(2,1)} %param.3) | data formatting | bytes 2097152 | tf_op args[0]
  2.6 0.0 copy-done
  2.6 0.0 copy-done.1
  2.6 84.5 %shard_map.50 = (bf16[8,16,32,128]{3,2,1,0:T(8,128)(2,1)S(1)}, f32[32,256]{1,0:T(8,128)S(1)}) custom-call(f32[3,14]{1,0:T(4,128)S(1)} %copy-done.1, bf16[8,16,32,128]{3,2,1,0:T(8,128)(2,1)S(1)} %bitcast.4, bf16[32,256]{1,0:T(8,128)(2,1)S(1)} %copy-done), custom_call_target="tpu_custom_call" | custom-call | tf_op jit(solution)/shard_map/pallas_call | solution.py:353
  87.1 1.4 %copy.6 = bf16[32,8,16,128]{3,2,1,0:T(8,128)(2,1)} copy(bf16[32,8,16,128]{3,0,2,1:T(8,128)(2,1)S(1)} %bitcast.5) | data formatting | bytes 2097152
  88.5 0.6 copy.10
Async XLA Ops:
  0.6 1.9 %copy-start = (bf16[32,256]{1,0:T(8,128)(2,1)S(1)}, bf16[32,256]{1,0:T(8,128)(2,1)}, u32[]{:S(2)}) copy-start(bf16[32,256]{1,0:T(8,128)(2,1)} %panels.1) | copy-start | bytes 49156
  0.6 1.9 %copy-start.1 = (f32[3,14]{1,0:T(4,128)S(1)}, f32[3,14]{1,0:T(4,128)}, u32[]{:S(2)}) copy-start(f32[3,14]{1,0:T(4,128)} %taps.1) | copy-start | bytes 508

commit v2 on v0

v2 whole, which is shorter than its diff:
```python
import functools

import jax
import jax.numpy as jnp
from jax import lax
from jax.experimental import pallas as pl
from jax.experimental.pallas import tpu as pltpu
from jax.sharding import PartitionSpec as P

MESH = pl.DeviceIdType.MESH
F32, BF16 = jnp.float32, jnp.bfloat16
BEFORE, AFTER = 7, 6
NY, NX = 4, 2
BAND = NY * NX
NG = 4
ZQ = 4
ORB, PLANES, ROWS, LANES = 32, 8, 16, 128
ALL = ORB * BAND
PAIR = 2
CHUNKS = PLANES // PAIR
SHARE = ROWS // BAND
FACE = 7
EIGHT = ORB // NG
STEPS = 3
SAME, CROSS = (4, 2, 6), (3, 5, 1, 7)


def band_matrix(taps, row):
    a = lax.broadcasted_iota(jnp.int32, (LANES, LANES), 0)
    b = lax.broadcasted_iota(jnp.int32, (LANES, LANES), 1)
    total = jnp.zeros((LANES, LANES), F32)
    for k in range(14):
        total = jnp.where(a - b == k - BEFORE, taps[row, k], total)
    high = total.astype(BF16)
    low = (total - high.astype(F32)).astype(BF16)
    return jnp.concatenate([high, low], axis=0)


def kernel(
    nz,
    taps, orbitals, panels,
    out, kin,
    psi, psi_p, far, near, acc, img, psi_all, img_all, rot, all_panels, kacc, ktwin, krs, kz1, kz2, kpart, zmat,
    part_send, part_recv, far_send, far_recv, near_send, near_recv, psi_send, psi_recv, pan_send, pan_recv,
    img_send, img_recv, rot_send, rot_recv, ktwin_send, ktwin_recv, krs_send, krs_recv, kz1_send, kz1_recv, kz2_send, kz2_recv, ka_send, ka_recv, known,
):
    band, space = lax.axis_index("band"), lax.axis_index("space")
    y, xl = band // NX, band % NX
    z, g, core = space // NG, space % NG, space % 2
    slabs = nz * NG
    partner = y * NX + (1 - xl)
    twin = space + 1 - 2 * core
    beyond = space - 1 + 2 * core
    inside = jnp.logical_and(beyond >= 0, beyond < slabs)
    layer = BAND * 2
    me = band * 2 + g // 2

    def remote(src, dst, send, recv, b, s):
        return pltpu.make_async_remote_copy(
            src_ref=src, dst_ref=dst, send_sem=send, recv_sem=recv, device_id=(b, s), device_id_type=MESH
        )

    def slot(b):
        return pl.ds(pl.multiple_of(b * ORB, ORB), ORB)

    def share(b):
        return pl.ds((b % NX) * (ROWS // NX) + (b // NX) * SHARE, SHARE)

    def peer(k):
        return lax.rem(band + k, BAND)

    barrier = pltpu.get_barrier_semaphore()

    def greet(b, s):
        pl.semaphore_signal(barrier, inc=1, device_id=(b, s), device_id_type=MESH)

    greet(partner, lax.rem(beyond + slabs, slabs))
    quarter, place = z // ZQ, z % ZQ
    quarters = nz // ZQ

    def z_near(k):
        return (quarter * ZQ + lax.rem(place + k, ZQ)) * NG + g

    def z_far(k):
        return (lax.rem(quarter + k, quarters) * ZQ + place) * NG + g

    def along(k):
        return lax.rem(z + k + nz, nz) * NG + g

    for k in (1, -1):
        greet(band, along(k))

    def in_layer(k):
        to = lax.rem(me + k, layer)
        return to, to // 2, z * NG + (to % 2) * 2 + core

    def greet_layer(k, carry):
        _, b, s = in_layer(k)
        greet(b, s)
        return carry

    lax.fori_loop(1, layer, greet_layer, 0)
    greet(band, twin)
    greet(band, z * NG + lax.rem(g + 2, NG) + 1 - 2 * core)
    size = ROWS * ROWS
    a = lax.broadcasted_iota(jnp.int32, (size, size), 0)
    b = lax.broadcasted_iota(jnp.int32, (size, size), 1)
    swap = jnp.where((a // ROWS == b % ROWS) & (a % ROWS == b // ROWS), 1.0, 0.0).astype(BF16)

    def turn(p, carry):
        for h in range(ORB // ROWS):
            v = orbitals[h * ROWS : (h + 1) * ROWS, p].reshape(size, LANES)
            r = jnp.dot(swap, v, preferred_element_type=F32).astype(BF16)
            psi[p, :, h * ROWS : (h + 1) * ROWS, :] = r.reshape(ROWS, ROWS, LANES)
        return carry

    lax.fori_loop(0, PLANES, turn, 0)
    pl.semaphore_wait(barrier, 1 + 2 + 2 + layer - 1)

    def tell(step):
        for k in (1 << step, -(1 << step)):
            pl.semaphore_signal(known.at[step], inc=1, device_id=(band, along(k)), device_id_type=MESH)

    def hear(step):
        pl.semaphore_wait(known.at[step], 2)

    tell(0)

    def plane(t):
        return t + core * (PLANES - 1 - 2 * t)

    def part_copy(t):
        p = plane(t)
        if t < FACE:
            return remote(psi.at[p], psi_p.at[p], part_send.at[t], part_recv.at[t], partner, space)
        rows = pl.ds((1 - xl) * (ROWS // NX), ROWS // NX)
        return remote(psi.at[p, rows], psi_p.at[p, rows], part_send.at[t], part_recv.at[t], partner, space)

    def far_copy(t):
        return remote(psi_p.at[plane(t)], far.at[t], far_send.at[t], far_recv.at[t], partner, beyond)

    near_copy = remote(psi.at[pl.ds(1 - core, FACE)], near, near_send, near_recv, band, twin)

    for t in range(PLANES):
        part_copy(t).start()
    near_copy.start()

    def psi_copy(k, h):
        to = lax.rem(y + k, NY) * NX + xl
        src, owner = (psi, band) if h == 0 else (psi_p, partner)
        planes = pl.ds(0, PLANES) if h == 0 else pl.ds(PLANES // 2 * (core if h == 1 else 1 - core), PLANES // 2)
        return remote(
            src.at[planes, share(to)], psi_all.at[planes, :, slot(owner), :],
            psi_send.at[k, h], psi_recv.at[k, h], to, space,
        )

    def panel_copy(k):
        return remote(panels, all_panels.at[slot(band), :], pan_send.at[k], pan_recv.at[k], peer(k), space)

    for k in (1, 3, 2):
        psi_copy(k, 0).start()
    all_panels[slot(band), :] = panels[...]
    psi_all[:, :, slot(band), :] = psi[:, share(band)]

    @pl.when(jnp.logical_not(inside))
    def _():
        far[...] = jnp.zeros(far.shape, BF16)

    def relay(t):
        part_copy(t).wait_recv()
        if t < FACE:

            @pl.when(inside)
            def _():
                far_copy(t).start()

    def arrived(t):
        @pl.when(inside)
        def _():
            far_copy(t).wait_recv()

    zmat[...] = band_matrix(taps, 2)

    def along_z(p, carry):
        v = psi[p].reshape(ROWS * ORB, LANES)
        r = jnp.dot(jnp.concatenate([v, v], axis=1), zmat[...], preferred_element_type=F32)
        acc[p] = r.reshape(ROWS, ORB, LANES)
        return carry

    lax.fori_loop(0, PLANES, along_z, 0)
    relay(0)
    half = 16

    def along_y(i, carry):
        p, h = i // 2, pl.ds(pl.multiple_of((i % 2) * half, half), half)
        v = [psi[p, r, h, :].astype(F32) for r in range(ROWS)]
        for r in range(ROWS):
            total = acc[p, r, h, :]
            for k in range(14):
                if 0 <= r + k - BEFORE < ROWS:
                    total = total + taps[1, k] * v[r + k - BEFORE]
            acc[p, r, h, :] = total
        return carry

    lax.fori_loop(0, PLANES * 2, along_y, 0)
    relay(1)

    def along_x(i, carry):
        r, h = i // 2, pl.ds(pl.multiple_of((i % 2) * half, half), half)
        v = [psi[q, r, h, :].astype(F32) for q in range(PLANES)]
        for p in range(PLANES):
            total = acc[p, r, h, :]
            for k in range(14):
                if 0 <= p + k - BEFORE < PLANES:
                    total = total + taps[0, k] * v[p + k - BEFORE]
            acc[p, r, h, :] = total
        return carry

    lax.fori_loop(0, ROWS * 2, along_x, 0)
    relay(2)

    def finish(planes, left, right):
        lefts = [q for q in range(BEFORE) if any(0 <= q - p < 14 for p in planes)]
        rights = [q for q in range(AFTER) if any(0 <= q + BEFORE + PLANES - p < 14 for p in planes)]

        def body(i, carry):
            r, h = i // 2, pl.ds(pl.multiple_of((i % 2) * half, half), half)
            lv = {q: left(q, r, h).astype(F32) for q in lefts}
            rv = {q: right(q, r, h).astype(F32) for q in rights}
            for p in planes:
                total = acc[p, r, h, :]
                for q in lefts:
                    if 0 <= q - p < 14:
                        total = total + taps[0, q - p] * lv[q]
                for q in rights:
                    k = q + BEFORE + PLANES - p
                    if 0 <= k < 14:
                        total = total + taps[0, k] * rv[q]
                img[p, r, h, :] = total.astype(BF16)
            return carry

        lax.fori_loop(0, ROWS * 2, body, 0)

    def pair(j):
        return pl.ds(PLANES - PAIR - PAIR * j + core * (2 * PAIR * j - PLANES + PAIR), PAIR)

    def img_copy(k, j):
        to = peer(k)
        return remote(
            img.at[pair(j), share(to)], img_all.at[pair(j), :, slot(band), :],
            img_send.at[k, j], img_recv.at[k, j], to, space,
        )

    def rot_copy(k, j):
        to = peer(k)
        return remote(
            rot.at[pair(j), :, slot(to), :], out.at[pair(j), share(band)],
            rot_send.at[k, j], rot_recv.at[k, j], to, space,
        )

    def image(j):
        @pl.when(core == 0)
        def _():
            finish(
                (PLANES - PAIR * (j + 1), PLANES - PAIR * j - 1),
                lambda q, r, h: far[BEFORE - 1 - q, r, h, :],
                lambda q, r, h: near[q, r, h, :],
            )

        @pl.when(core == 1)
        def _():
            finish(
                (PAIR * j, PAIR * j + 1),
                lambda q, r, h: near[q, r, h, :],
                lambda q, r, h: far[q, r, h, :],
            )

        for k in SAME:
            img_copy(k, j).start()
        img_all[pair(j), :, slot(band), :] = img[pair(j), share(band)]

    def spread(ref, j):
        v = ref[pair(j)]
        return jnp.concatenate([v[a, b] for a in range(PAIR) for b in range(SHARE)], axis=1)

    def rotate(j):
        r = jnp.dot(all_panels[...], spread(img_all, j), preferred_element_type=F32).astype(BF16)
        parts = [r[:, i * LANES : (i + 1) * LANES] for i in range(PAIR * SHARE)]
        rot[pair(j)] = jnp.stack(parts).reshape(PAIR, SHARE, ALL, LANES)

    def kinetic(j):
        r = lax.dot_general(
            spread(psi_all, j), spread(img_all, j), (((1,), (1,)), ((), ())), preferred_element_type=F32
        ).reshape(kacc.shape)
        kacc[...] = r if j == 0 else kacc[...] + r

    near_copy.wait_recv()
    hear(0)
    tell(1)
    arrived(0)
    image(0)
    relay(3)
    for k in (1, 3, 2):
        psi_copy(k, 1).start()
    relay(4)
    hear(1)
    tell(2)
    arrived(1)
    arrived(2)
    image(1)
    relay(5)
    relay(6)
    arrived(3)
    arrived(4)
    image(2)
    relay(7)
    for k in (1, 3, 2):
        psi_copy(k, 2).start()
    for t in range(PLANES):
        part_copy(t).wait_send()
    for j in range(CHUNKS - 1):
        for k in CROSS:
            img_copy(k, j).start()
    psi_all[:, :, slot(partner), :] = psi_p[:, share(band)]
    arrived(5)
    arrived(6)
    image(3)
    for k in CROSS:
        img_copy(k, CHUNKS - 1).start()
    for k in SAME + CROSS:
        panel_copy(k).start()

    for k in range(1, NY):
        for h in range(3):
            psi_copy(k, h).wait_recv()
    for j in range(CHUNKS):
        for k in range(1, BAND):
            img_copy(k, j).wait_recv()
        kinetic(j)

    def krs_copy(k):
        to, b, s = in_layer(k)
        return remote(ktwin.at[to], krs.at[k], krs_send.at[k], krs_recv.at[k], b, s)

    twin_copy = remote(kacc.at[:, 1 - core], ktwin, ktwin_send, ktwin_recv, band, twin)
    twin_copy.start()
    twin_copy.wait_recv()
    ktwin[...] += kacc[:, core]

    def krs_start(k, carry):
        krs_copy(k).start()
        return carry

    def krs_wait(k, carry):
        krs_copy(k).wait_recv()
        return carry

    lax.fori_loop(1, layer, krs_start, 0)


    def cross(j):
        for k in CROSS:
            rot_copy(k, j).start()

    for k in range(1, BAND):
        panel_copy(k).wait_recv()
    for j in range(CHUNKS):
        rotate(j)
        for k in SAME:
            rot_copy(k, j).start()
        if j < 2:
            cross(j)
    for j in range(CHUNKS):
        out[pair(j), share(band)] = rot[pair(j), :, slot(band), :]
    krs[0] = ktwin[me]
    lax.fori_loop(1, layer, krs_wait, 0)
    scale = 1.0 / (slabs * PLANES * ROWS * LANES)
    kpart[0] = jnp.sum(krs[...], axis=0) * scale

    def kz1_copy(k):
        return remote(kpart.at[0], kz1.at[place], kz1_send.at[k], kz1_recv.at[k], band, z_near(k))

    def kz2_copy(k):
        return remote(kpart.at[1], kz2.at[quarter], kz2_send.at[k], kz2_recv.at[k], band, z_far(k))

    hear(2)
    for k in range(1, ZQ):
        kz1_copy(k).start()
    cross(2)
    kz1[place] = kpart[0]
    for k in range(1, ZQ):
        kz1_copy(k).wait_recv()
    kpart[1] = jnp.sum(kz1[...], axis=0)
    for k in range(1, quarters):
        kz2_copy(k).start()
    cross(3)
    kz2[quarter] = kpart[1]
    for k in range(1, quarters):
        kz2_copy(k).wait_recv()
    rows = pl.ds(pl.multiple_of(g * EIGHT, EIGHT), EIGHT)
    kin[rows, :] = jnp.sum(kz2[...], axis=0)

    def ka_copy(k):
        return remote(
            kin.at[rows, :], kin.at[rows, :], ka_send.at[k], ka_recv.at[k], band, z * NG + lax.rem(g + k, NG)
        )

    for k in range(1, NG):
        ka_copy(k).start()
    for k in range(1, NG):
        ka_copy(k).wait_recv()
    for j in range(CHUNKS):
        for k in range(1, BAND):
            rot_copy(k, j).wait_recv()

    @pl.when(inside)
    def _():
        for t in range(FACE):
            far_copy(t).wait_send()

    near_copy.wait_send()
    for k in range(1, NY):
        for h in range(3):
            psi_copy(k, h).wait_send()
    for k in range(1, BAND):
        panel_copy(k).wait_send()
        for j in range(CHUNKS):
            img_copy(k, j).wait_send()
            rot_copy(k, j).wait_send()

    def krs_sent(k, carry):
        krs_copy(k).wait_send()
        return carry

    twin_copy.wait_send()
    lax.fori_loop(1, layer, krs_sent, 0)
    for k in range(1, ZQ):
        kz1_copy(k).wait_send()
    for k in range(1, quarters):
        kz2_copy(k).wait_send()
    for k in range(1, NG):
        ka_copy(k).wait_send()


def on_device(nz, orbitals, filters, panels):
    vmem = pltpu.VMEM
    dma = pltpu.SemaphoreType.DMA
    slab = (PLANES, ROWS, ORB, LANES)
    mixed = (PLANES, SHARE, ALL, LANES)
    layer = BAND * 2
    rotated, kin = pl.pallas_call(
        functools.partial(kernel, nz),
        out_shape=(jax.ShapeDtypeStruct(slab, BF16), jax.ShapeDtypeStruct((ORB, ALL), F32)),
        in_specs=[
            pl.BlockSpec(memory_space=pltpu.SMEM),
            pl.BlockSpec(memory_space=vmem),
            pl.BlockSpec(memory_space=vmem),
        ],
        out_specs=(pl.BlockSpec(memory_space=vmem), pl.BlockSpec(memory_space=vmem)),
        scratch_shapes=[
            vmem(slab, BF16),
            vmem(slab, BF16),
            vmem((FACE, ROWS, ORB, LANES), BF16),
            vmem((FACE, ROWS, ORB, LANES), BF16),
            vmem(slab, F32),
            vmem(slab, BF16),
            vmem(mixed, BF16),
            vmem(mixed, BF16),
            vmem(mixed, BF16),
            vmem((ALL, ALL), BF16),
            vmem((BAND * 2, 2, EIGHT, ALL), F32),
            vmem((BAND * 2, EIGHT, ALL), F32),
            vmem((layer, EIGHT, ALL), F32),
            vmem((ZQ, EIGHT, ALL), F32),
            vmem((nz // ZQ, EIGHT, ALL), F32),
            vmem((2, EIGHT, ALL), F32),
            vmem((2 * LANES, LANES), BF16),
            dma((PLANES,)), dma((PLANES,)),
            dma((FACE,)), dma((FACE,)),
            dma, dma,
            dma((NY, 3)), dma((NY, 3)),
            dma((BAND,)), dma((BAND,)),
            dma((BAND, CHUNKS)), dma((BAND, CHUNKS)),
            dma((BAND, CHUNKS)), dma((BAND, CHUNKS)),
            dma, dma,
            dma((layer,)), dma((layer,)),
            dma((ZQ,)), dma((ZQ,)),
            dma((nz // ZQ,)), dma((nz // ZQ,)),
            dma((NG,)), dma((NG,)),
            pltpu.SemaphoreType.REGULAR((STEPS,)),
        ],
        compiler_params=pltpu.CompilerParams(
            collective_id=0, has_side_effects=True, vmem_limit_bytes=40 * 1024 * 1024
        ),
    )(filters, orbitals, panels)
    return jnp.transpose(rotated, (2, 0, 1, 3)), kin


def solution(mesh):
    return jax.shard_map(
        functools.partial(on_device, mesh.shape["space"] // NG),
        mesh=mesh,
        in_specs=(P("band", "space", None, None), P(), P("band", None)),
        out_specs=(P("band", "space", None, None), P("band", None)),
        check_vma=False,
    )
```

time: 542 us -> 80.8 us (0.15)
  blocking collectives: 256 us -> 0 us
  waiting for transfers between devices: 195 us -> 0 us
  Pallas kernels: 0 us -> 75.3 us
  other arithmetic: 35 us -> 0 us
  between operations: 14.1 us -> 0.65 us
  local copies, waits for them, and re-layouts: 17.3 us -> 4.61 us
  starting transfers between devices: 10.2 us -> 0 us
  matrix products: 8.65 us -> 0 us
    psum x1 -> x0, blocking collectives: 256 us -> none  [on_device(): kin_rows = lax.psum(kin_rows * scale, 'space')]
    all_gather x1 -> x0, waiting for transfers between devices: 181 us -> none  [on_device(): piece = lax.all_gather(image, 'band', axis=0, tiled=True)]
    pallas_call x0 -> x1, Pallas kernels: none -> 75.3 us  [on_device(): pl.pallas_call(functools.partial(kernel, nz), out_shape=(jax.ShapeDtypeSt...]
    convert_element_type x2 -> x0, other arithmetic: 35 us -> none  [the longest x1 34.6 us: on_device(): (along_x + local_pass(inner, filters[1], 2) + local_pass(inner, filters[2...]
    ppermute x2 -> x0, waiting for transfers between devices: 13.9 us -> none  [the longest x1 13.9 us: extended(): before = lax.ppermute(last, axis, up)]
    all_gather x1 -> x0, local copies, waits for them, and re-layouts: 11.4 us -> none  [on_device(): piece = lax.all_gather(image, 'band', axis=0, tiled=True)]
    ppermute x2 -> x0, starting transfers between devices: 10.1 us -> none  [the longest x1 6.04 us: extended(): before = lax.ppermute(last, axis, up)]
    dot_general x2 -> x0, matrix products: 8.65 us -> none  [the longest x1 6.05 us: on_device(): rot_sum = jnp.dot(panels, flat, preferred_element_type=jnp.float32)]
  transfers between devices with their start and end apart: 3 -> 0, of which waited for: 2 -> 0; matrix products, arithmetic and copies ran while one was open for 0% -> 0% of each run, Pallas kernels for 0% -> 0%
where the time goes in v2:
time: 80.8 us; the launch traced here: 80.5 us
  Pallas kernels  75.3 us (93%)
  local copies, waits for them, and re-layouts  4.61 us (6%)
    pallas_call x1, Pallas kernels, on_device(): pl.pallas_call(functools.partial(kernel, nz), out_shape=(jax.ShapeDtypeSt...  75.3 us
    unnamed x8, local copies, waits for them, and re-layouts  4.61 us

profile of v2, /device:TPU:1, one launch (start us, length us, event | category | flops | bytes accessed | tf_op | source)
XLA Modules:
  0.0 80.5 jit_solution(13399369826179299216)
XLA Ops:
  0.6 0.0 copy-start
  0.6 1.2 %copy-done = bf16[32,8,16,128]{3,2,1,0:T(8,128)(2,1)S(1)} copy-done((bf16[32,8,16,128]{3,2,1,0:T(8,128)(2,1)S(1)}, bf16[32,8,16,128]{3,2,1,0:T(8,128)(2,1)}, u32[]{:S(2)}) %copy-start) | copy-done | bytes 1048600
  1.9 0.0 copy-start.1
  1.9 0.7 copy-done.1
  2.6 0.0 copy-start.2
  2.6 0.7 copy-done.2
  3.3 75.3 %shard_map.50 = (bf16[8,16,32,128]{3,2,1,0:T(8,128)(2,1)S(1)}, f32[32,256]{1,0:T(8,128)S(1)}) custom-call(f32[3,14]{1,0:T(4,128)S(1)} %copy-done.2, bf16[32,8,16,128]{3,2,1,0:T(8,128)(2,1)S(1)} %copy-done, bf16[32,256]{1,0:T(8,128)(2,1)S(1)} %copy-done.1), custom_call_target="tpu_custom_call" | custom-call | tf_op jit(solution)/shard_map/pallas_call | solution.py:451
  78.5 1.4 %copy.5 = bf16[32,8,16,128]{3,2,1,0:T(8,128)(2,1)} copy(bf16[32,8,16,128]{3,0,2,1:T(8,128)(2,1)S(1)} %bitcast.1) | data formatting | bytes 2097152
  79.9 0.6 copy.7
Async XLA Ops:
  0.6 1.2 %copy-start = (bf16[32,8,16,128]{3,2,1,0:T(8,128)(2,1)S(1)}, bf16[32,8,16,128]{3,2,1,0:T(8,128)(2,1)}, u32[]{:S(2)}) copy-start(bf16[32,8,16,128]{3,2,1,0:T(8,128)(2,1)} %orbitals.1) | copy-start | bytes 3145732
  1.9 0.7 copy-start.1
  2.6 0.7 copy-start.2

commit v3 on v2

--- a/solution.py
+++ b/solution.py
@@ -16,8 +16,8 @@
 ZQ = 4
 ORB, PLANES, ROWS, LANES = 32, 8, 16, 128
 ALL = ORB * BAND
-PAIR = 2
-CHUNKS = PLANES // PAIR
+SIZES = (2, 2, 2, 1, 1)
+CHUNKS = len(SIZES)
 SHARE = ROWS // BAND
 FACE = 7
 EIGHT = ORB // NG
@@ -148,7 +148,8 @@
     def psi_copy(k, h):
         to = lax.rem(y + k, NY) * NX + xl
         src, owner = (psi, band) if h == 0 else (psi_p, partner)
-        planes = pl.ds(0, PLANES) if h == 0 else pl.ds(PLANES // 2 * (core if h == 1 else 1 - core), PLANES // 2)
+        first, count = ((0, PLANES), (0, 4), (4, 2), (6, 2))[h]
+        planes = pl.ds(first + core * (PLANES - count - 2 * first), count) if h else pl.ds(0, PLANES)
         return remote(
             src.at[planes, share(to)], psi_all.at[planes, :, slot(owner), :],
             psi_send.at[k, h], psi_recv.at[k, h], to, space,
@@ -242,7 +243,8 @@
         lax.fori_loop(0, ROWS * 2, body, 0)
 
     def pair(j):
-        return pl.ds(PLANES - PAIR - PAIR * j + core * (2 * PAIR * j - PLANES + PAIR), PAIR)
+        done, count = sum(SIZES[:j]), SIZES[j]
+        return pl.ds(PLANES - done - count + core * (2 * done + count - PLANES), count)
 
     def img_copy(k, j):
         to = peer(k)
@@ -262,7 +264,7 @@
         @pl.when(core == 0)
         def _():
             finish(
-                (PLANES - PAIR * (j + 1), PLANES - PAIR * j - 1),
+                range(PLANES - sum(SIZES[: j + 1]), PLANES - sum(SIZES[:j])),
                 lambda q, r, h: far[BEFORE - 1 - q, r, h, :],
                 lambda q, r, h: near[q, r, h, :],
             )
@@ -270,23 +272,23 @@
         @pl.when(core == 1)
         def _():
             finish(
-                (PAIR * j, PAIR * j + 1),
+                range(sum(SIZES[:j]), sum(SIZES[: j + 1])),
                 lambda q, r, h: near[q, r, h, :],
                 lambda q, r, h: far[q, r, h, :],
             )
 
-        for k in SAME:
+        for k in SAME + CROSS:
             img_copy(k, j).start()
         img_all[pair(j), :, slot(band), :] = img[pair(j), share(band)]
 
     def spread(ref, j):
         v = ref[pair(j)]
-        return jnp.concatenate([v[a, b] for a in range(PAIR) for b in range(SHARE)], axis=1)
+        return jnp.concatenate([v[a, b] for a in range(SIZES[j]) for b in range(SHARE)], axis=1)
 
     def rotate(j):
         r = jnp.dot(all_panels[...], spread(img_all, j), preferred_element_type=F32).astype(BF16)
-        parts = [r[:, i * LANES : (i + 1) * LANES] for i in range(PAIR * SHARE)]
-        rot[pair(j)] = jnp.stack(parts).reshape(PAIR, SHARE, ALL, LANES)
+        parts = [r[:, i * LANES : (i + 1) * LANES] for i in range(SIZES[j] * SHARE)]
+        rot[pair(j)] = jnp.stack(parts).reshape(SIZES[j], SHARE, ALL, LANES)
 
     def kinetic(j):
         r = lax.dot_general(
@@ -295,43 +297,39 @@
         kacc[...] = r if j == 0 else kacc[...] + r
 
     near_copy.wait_recv()
-    hear(0)
-    tell(1)
     arrived(0)
     image(0)
     relay(3)
     for k in (1, 3, 2):
         psi_copy(k, 1).start()
     relay(4)
-    hear(1)
-    tell(2)
     arrived(1)
     arrived(2)
     image(1)
+    hear(0)
+    tell(1)
     relay(5)
     relay(6)
+    for k in (1, 3, 2):
+        psi_copy(k, 2).start()
     arrived(3)
     arrived(4)
     image(2)
     relay(7)
     for k in (1, 3, 2):
-        psi_copy(k, 2).start()
-    for t in range(PLANES):
-        part_copy(t).wait_send()
-    for j in range(CHUNKS - 1):
-        for k in CROSS:
-            img_copy(k, j).start()
+        psi_copy(k, 3).start()
     psi_all[:, :, slot(partner), :] = psi_p[:, share(band)]
     arrived(5)
+    image(3)
     arrived(6)
-    image(3)
-    for k in CROSS:
-        img_copy(k, CHUNKS - 1).start()
+    image(4)
+    hear(1)
+    tell(2)
     for k in SAME + CROSS:
         panel_copy(k).start()
 
     for k in range(1, NY):
-        for h in range(3):
+        for h in range(4):
             psi_copy(k, h).wait_recv()
     for j in range(CHUNKS):
         for k in range(1, BAND):
@@ -358,20 +356,17 @@
     lax.fori_loop(1, layer, krs_start, 0)
 
 
-    def cross(j):
-        for k in CROSS:
-            rot_copy(k, j).start()
-
     for k in range(1, BAND):
         panel_copy(k).wait_recv()
-    for j in range(CHUNKS):
+
+    def turn_out(j):
         rotate(j)
-        for k in SAME:
+        for k in SAME + CROSS:
             rot_copy(k, j).start()
-        if j < 2:
-            cross(j)
-    for j in range(CHUNKS):
         out[pair(j), share(band)] = rot[pair(j), :, slot(band), :]
+
+    turn_out(0)
+    turn_out(1)
     krs[0] = ktwin[me]
     lax.fori_loop(1, layer, krs_wait, 0)
     scale = 1.0 / (slabs * PLANES * ROWS * LANES)
@@ -386,14 +381,15 @@
     hear(2)
     for k in range(1, ZQ):
         kz1_copy(k).start()
-    cross(2)
+    turn_out(2)
     kz1[place] = kpart[0]
     for k in range(1, ZQ):
         kz1_copy(k).wait_recv()
     kpart[1] = jnp.sum(kz1[...], axis=0)
     for k in range(1, quarters):
         kz2_copy(k).start()
-    cross(3)
+    turn_out(3)
+    turn_out(4)
     kz2[quarter] = kpart[1]
     for k in range(1, quarters):
         kz2_copy(k).wait_recv()
@@ -413,6 +409,8 @@
         for k in range(1, BAND):
             rot_copy(k, j).wait_recv()
 
+    for t in range(PLANES):
+        part_copy(t).wait_send()
     @pl.when(inside)
     def _():
         for t in range(FACE):
@@ -420,7 +418,7 @@
 
     near_copy.wait_send()
     for k in range(1, NY):
-        for h in range(3):
+        for h in range(4):
             psi_copy(k, h).wait_send()
     for k in range(1, BAND):
         panel_copy(k).wait_send()
@@ -478,7 +476,7 @@
             dma((PLANES,)), dma((PLANES,)),
             dma((FACE,)), dma((FACE,)),
             dma, dma,
-            dma((NY, 3)), dma((NY, 3)),
+            dma((NY, 4)), dma((NY, 4)),
             dma((BAND,)), dma((BAND,)),
             dma((BAND, CHUNKS)), dma((BAND, CHUNKS)),
             dma((BAND, CHUNKS)), dma((BAND, CHUNKS)),

time: 80.8 us -> 79.8 us (0.988)
  Pallas kernels: 75.3 us -> 74.3 us
    pallas_call x1, Pallas kernels: 75.3 us -> 74.3 us  [on_device(): pl.pallas_call(functools.partial(kernel, nz), out_shape=(jax.ShapeDtypeSt...]
where the time goes in v3:
time: 79.8 us; the launch traced here: 79.6 us
  Pallas kernels  74.3 us (93%)
  local copies, waits for them, and re-layouts  4.61 us (6%)
    pallas_call x1, Pallas kernels, on_device(): pl.pallas_call(functools.partial(kernel, nz), out_shape=(jax.ShapeDtypeSt...  74.3 us
    unnamed x8, local copies, waits for them, and re-layouts  4.61 us

profile of v3, /device:TPU:1, one launch (start us, length us, event | category | flops | bytes accessed | tf_op | source)
XLA Modules:
  0.0 79.6 jit_solution(13388555654987518108)
XLA Ops:
  0.6 0.0 copy-start
  0.6 1.2 %copy-done = bf16[32,8,16,128]{3,2,1,0:T(8,128)(2,1)S(1)} copy-done((bf16[32,8,16,128]{3,2,1,0:T(8,128)(2,1)S(1)}, bf16[32,8,16,128]{3,2,1,0:T(8,128)(2,1)}, u32[]{:S(2)}) %copy-start) | copy-done | bytes 1048600
  1.9 0.0 copy-start.1
  1.9 0.7 copy-done.1
  2.6 0.0 copy-start.2
  2.6 0.7 copy-done.2
  3.3 74.3 %shard_map.50 = (bf16[8,16,32,128]{3,2,1,0:T(8,128)(2,1)S(1)}, f32[32,256]{1,0:T(8,128)S(1)}) custom-call(f32[3,14]{1,0:T(4,128)S(1)} %copy-done.2, bf16[32,8,16,128]{3,2,1,0:T(8,128)(2,1)S(1)} %copy-done, bf16[32,256]{1,0:T(8,128)(2,1)S(1)} %copy-done.1), custom_call_target="tpu_custom_call" | custom-call | tf_op jit(solution)/shard_map/pallas_call | solution.py:449
  77.6 1.4 %copy.5 = bf16[32,8,16,128]{3,2,1,0:T(8,128)(2,1)} copy(bf16[32,8,16,128]{3,0,2,1:T(8,128)(2,1)S(1)} %bitcast.1) | data formatting | bytes 2097152
  79.0 0.6 copy.7
Async XLA Ops:
  0.6 1.2 %copy-start = (bf16[32,8,16,128]{3,2,1,0:T(8,128)(2,1)S(1)}, bf16[32,8,16,128]{3,2,1,0:T(8,128)(2,1)}, u32[]{:S(2)}) copy-start(bf16[32,8,16,128]{3,2,1,0:T(8,128)(2,1)} %orbitals.1) | copy-start | bytes 3145732
  1.9 0.7 copy-start.1
  2.6 0.7 copy-start.2

commit v4 on v3

--- a/solution.py
+++ b/solution.py
@@ -13,7 +13,6 @@
 NY, NX = 4, 2
 BAND = NY * NX
 NG = 4
-ZQ = 4
 ORB, PLANES, ROWS, LANES = 32, 8, 16, 128
 ALL = ORB * BAND
 SIZES = (2, 2, 2, 1, 1)
@@ -38,11 +37,11 @@
 
 def kernel(
     nz,
-    taps, orbitals, panels,
+    taps, orbitals_in, panels_in,
     out, kin,
-    psi, psi_p, far, near, acc, img, psi_all, img_all, rot, all_panels, kacc, ktwin, krs, kz1, kz2, kpart, zmat,
+    orbitals, panels, psi, psi_p, far, near, acc, img, psi_all, img_all, rot, all_panels, kacc, ktwin, krs, kz, kpart, zmat,
     part_send, part_recv, far_send, far_recv, near_send, near_recv, psi_send, psi_recv, pan_send, pan_recv,
-    img_send, img_recv, rot_send, rot_recv, ktwin_send, ktwin_recv, krs_send, krs_recv, kz1_send, kz1_recv, kz2_send, kz2_recv, ka_send, ka_recv, known,
+    img_send, img_recv, rot_send, rot_recv, ktwin_send, ktwin_recv, krs_send, krs_recv, kz_send, kz_recv, ka_send, ka_recv, known, load, keep,
 ):
     band, space = lax.axis_index("band"), lax.axis_index("space")
     y, xl = band // NX, band % NX
@@ -69,21 +68,19 @@
     def peer(k):
         return lax.rem(band + k, BAND)
 
+    loads = [
+        pltpu.make_async_copy(orbitals_in, orbitals, load.at[0]),
+        pltpu.make_async_copy(panels_in, panels, load.at[1]),
+    ]
+    for copy in loads:
+        copy.start()
+
     barrier = pltpu.get_barrier_semaphore()
 
     def greet(b, s):
         pl.semaphore_signal(barrier, inc=1, device_id=(b, s), device_id_type=MESH)
 
     greet(partner, lax.rem(beyond + slabs, slabs))
-    quarter, place = z // ZQ, z % ZQ
-    quarters = nz // ZQ
-
-    def z_near(k):
-        return (quarter * ZQ + lax.rem(place + k, ZQ)) * NG + g
-
-    def z_far(k):
-        return (lax.rem(quarter + k, quarters) * ZQ + place) * NG + g
-
     def along(k):
         return lax.rem(z + k + nz, nz) * NG + g
 
@@ -114,7 +111,9 @@
             psi[p, :, h * ROWS : (h + 1) * ROWS, :] = r.reshape(ROWS, ROWS, LANES)
         return carry
 
+    loads[0].wait()
     lax.fori_loop(0, PLANES, turn, 0)
+    loads[1].wait()
     pl.semaphore_wait(barrier, 1 + 2 + 2 + layer - 1)
 
     def tell(step):
@@ -259,6 +258,9 @@
             rot.at[pair(j), :, slot(to), :], out.at[pair(j), share(band)],
             rot_send.at[k, j], rot_recv.at[k, j], to, space,
         )
+
+    def keep_copy(j):
+        return pltpu.make_async_copy(rot.at[pair(j), :, slot(band), :], out.at[pair(j), share(band)], keep.at[j])
 
     def image(j):
         @pl.when(core == 0)
@@ -345,15 +347,8 @@
     twin_copy.wait_recv()
     ktwin[...] += kacc[:, core]
 
-    def krs_start(k, carry):
+    for k in sorted(range(1, layer), key=lambda k: -min(k, layer - k)):
         krs_copy(k).start()
-        return carry
-
-    def krs_wait(k, carry):
-        krs_copy(k).wait_recv()
-        return carry
-
-    lax.fori_loop(1, layer, krs_start, 0)
 
 
     for k in range(1, BAND):
@@ -363,38 +358,31 @@
         rotate(j)
         for k in SAME + CROSS:
             rot_copy(k, j).start()
-        out[pair(j), share(band)] = rot[pair(j), :, slot(band), :]
+        keep_copy(j).start()
 
     turn_out(0)
     turn_out(1)
     krs[0] = ktwin[me]
-    lax.fori_loop(1, layer, krs_wait, 0)
+    for k in range(1, layer):
+        krs_copy(k).wait_recv()
     scale = 1.0 / (slabs * PLANES * ROWS * LANES)
-    kpart[0] = jnp.sum(krs[...], axis=0) * scale
-
-    def kz1_copy(k):
-        return remote(kpart.at[0], kz1.at[place], kz1_send.at[k], kz1_recv.at[k], band, z_near(k))
-
-    def kz2_copy(k):
-        return remote(kpart.at[1], kz2.at[quarter], kz2_send.at[k], kz2_recv.at[k], band, z_far(k))
+    kpart[...] = jnp.sum(krs[...], axis=0) * scale
+
+    def kz_copy(k):
+        return remote(kpart, kz.at[z], kz_send.at[k], kz_recv.at[k], band, along(k))
 
     hear(2)
-    for k in range(1, ZQ):
-        kz1_copy(k).start()
+    far_first = sorted(range(1, nz), key=lambda k: -min(k, nz - k))
+    for k in far_first:
+        kz_copy(k).start()
     turn_out(2)
-    kz1[place] = kpart[0]
-    for k in range(1, ZQ):
-        kz1_copy(k).wait_recv()
-    kpart[1] = jnp.sum(kz1[...], axis=0)
-    for k in range(1, quarters):
-        kz2_copy(k).start()
     turn_out(3)
     turn_out(4)
-    kz2[quarter] = kpart[1]
-    for k in range(1, quarters):
-        kz2_copy(k).wait_recv()
+    kz[z] = kpart[...]
+    for k in far_first:
+        kz_copy(k).wait_recv()
     rows = pl.ds(pl.multiple_of(g * EIGHT, EIGHT), EIGHT)
-    kin[rows, :] = jnp.sum(kz2[...], axis=0)
+    kin[rows, :] = jnp.sum(kz[...], axis=0)
 
     def ka_copy(k):
         return remote(
@@ -409,6 +397,8 @@
         for k in range(1, BAND):
             rot_copy(k, j).wait_recv()
 
+    for j in range(CHUNKS):
+        keep_copy(j).wait()
     for t in range(PLANES):
         part_copy(t).wait_send()
     @pl.when(inside)
@@ -432,10 +422,8 @@
 
     twin_copy.wait_send()
     lax.fori_loop(1, layer, krs_sent, 0)
-    for k in range(1, ZQ):
-        kz1_copy(k).wait_send()
-    for k in range(1, quarters):
-        kz2_copy(k).wait_send()
+    for k in range(1, nz):
+        kz_copy(k).wait_send()
     for k in range(1, NG):
         ka_copy(k).wait_send()
 
@@ -451,11 +439,13 @@
         out_shape=(jax.ShapeDtypeStruct(slab, BF16), jax.ShapeDtypeStruct((ORB, ALL), F32)),
         in_specs=[
             pl.BlockSpec(memory_space=pltpu.SMEM),
-            pl.BlockSpec(memory_space=vmem),
-            pl.BlockSpec(memory_space=vmem),
+            pl.BlockSpec(memory_space=pl.ANY),
+            pl.BlockSpec(memory_space=pl.ANY),
         ],
-        out_specs=(pl.BlockSpec(memory_space=vmem), pl.BlockSpec(memory_space=vmem)),
+        out_specs=(pl.BlockSpec(memory_space=pl.ANY), pl.BlockSpec(memory_space=vmem)),
         scratch_shapes=[
+            vmem((ORB, PLANES, ROWS, LANES), BF16),
+            vmem((ORB, ALL), BF16),
             vmem(slab, BF16),
             vmem(slab, BF16),
             vmem((FACE, ROWS, ORB, LANES), BF16),
@@ -469,9 +459,8 @@
             vmem((BAND * 2, 2, EIGHT, ALL), F32),
             vmem((BAND * 2, EIGHT, ALL), F32),
             vmem((layer, EIGHT, ALL), F32),
-            vmem((ZQ, EIGHT, ALL), F32),
-            vmem((nz // ZQ, EIGHT, ALL), F32),
-            vmem((2, EIGHT, ALL), F32),
+            vmem((nz, EIGHT, ALL), F32),
+            vmem((EIGHT, ALL), F32),
             vmem((2 * LANES, LANES), BF16),
             dma((PLANES,)), dma((PLANES,)),
             dma((FACE,)), dma((FACE,)),
@@ -482,13 +471,14 @@
             dma((BAND, CHUNKS)), dma((BAND, CHUNKS)),
             dma, dma,
             dma((layer,)), dma((layer,)),
-            dma((ZQ,)), dma((ZQ,)),
-            dma((nz // ZQ,)), dma((nz // ZQ,)),
+            dma((nz,)), dma((nz,)),
             dma((NG,)), dma((NG,)),
             pltpu.SemaphoreType.REGULAR((STEPS,)),
+            dma((2,)),
+            dma((CHUNKS,)),
         ],
         compiler_params=pltpu.CompilerParams(
-            collective_id=0, has_side_effects=True, vmem_limit_bytes=40 * 1024 * 1024
+            collective_id=0, has_side_effects=True, vmem_limit_bytes=57344 * 1024
         ),
     )(filters, orbitals, panels)
     return jnp.transpose(rotated, (2, 0, 1, 3)), kin

time: 79.8 us -> 77.7 us (0.974)
  local copies, waits for them, and re-layouts: 4.61 us -> 3.23 us
    unnamed x8 -> x4, local copies, waits for them, and re-layouts: 4.61 us -> 3.23 us
where the time goes in v4:
time: 77.7 us; the launch traced here: 77.6 us
  Pallas kernels  73.7 us (95%)
  local copies, waits for them, and re-layouts  3.23 us (4%)
    pallas_call x1, Pallas kernels, on_device(): pl.pallas_call(functools.partial(kernel, nz), out_shape=(jax.ShapeDtypeSt...  73.7 us
    unnamed x4, local copies, waits for them, and re-layouts  3.23 us

profile of v4, /device:TPU:1, one launch (start us, length us, event | category | flops | bytes accessed | tf_op | source)
XLA Modules:
  0.0 77.6 jit_solution(10160437768457858786)
XLA Ops:
  0.6 73.7 %shard_map.50 = (bf16[8,16,32,128]{3,2,1,0:T(8,128)(2,1)}, f32[32,256]{1,0:T(8,128)}) custom-call(f32[3,14]{1,0:T(4,128)} %taps.1, bf16[32,8,16,128]{3,2,1,0:T(8,128)(2,1)} %orbitals_in.1, bf16[32,256]{1,0:T(8,128)(2,1)} %panels_in.1), custom_call_target="tpu_custom_call" | custom-call | tf_op jit(solution)/shard_map/pallas_call | solution.py:437
  74.3 0.0 copy-start
  74.3 2.6 %copy.5 = bf16[32,8,16,128]{3,2,1,0:T(8,128)(2,1)} copy(bf16[32,8,16,128]{3,0,2,1:T(8,128)(2,1)} %bitcast.1) | data formatting | bytes 2097152
  76.9 0.0 copy-done
  76.9 0.6 copy.7
Async XLA Ops:
  74.3 2.6 %copy-start = (f32[32,256]{1,0:T(8,128)S(1)}, f32[32,256]{1,0:T(8,128)}, u32[]{:S(2)}) copy-start(f32[32,256]{1,0:T(8,128)} %get-tuple-element.11) | copy-start | bytes 98308

commit v5 on v4

--- a/solution.py
+++ b/solution.py
@@ -170,12 +170,12 @@
         part_copy(t).wait_recv()
         if t < FACE:
 
-            @pl.when(inside)
+            @pl.when(inside if t < AFTER else jnp.logical_and(inside, core == 1))
             def _():
                 far_copy(t).start()
 
     def arrived(t):
-        @pl.when(inside)
+        @pl.when(inside if t < AFTER else jnp.logical_and(inside, core == 0))
         def _():
             far_copy(t).wait_recv()
 
@@ -403,8 +403,12 @@
         part_copy(t).wait_send()
     @pl.when(inside)
     def _():
-        for t in range(FACE):
+        for t in range(AFTER):
             far_copy(t).wait_send()
+
+    @pl.when(jnp.logical_and(inside, core == 1))
+    def _():
+        far_copy(AFTER).wait_send()
 
     near_copy.wait_send()
     for k in range(1, NY):

time: 77.7 us -> 77.7 us (level)
  no operation moved by 1% of the time
where the time goes in v5:
time: 77.7 us; the launch traced here: 77.5 us
  Pallas kernels  73.6 us (95%)
  local copies, waits for them, and re-layouts  3.23 us (4%)
    pallas_call x1, Pallas kernels, on_device(): pl.pallas_call(functools.partial(kernel, nz), out_shape=(jax.ShapeDtypeSt...  73.6 us
    unnamed x4, local copies, waits for them, and re-layouts  3.23 us

profile of v5, /device:TPU:1, one launch (start us, length us, event | category | flops | bytes accessed | tf_op | source)
XLA Modules:
  0.0 77.5 jit_solution(11610919566709008800)
XLA Ops:
  0.6 73.6 %shard_map.50 = (bf16[8,16,32,128]{3,2,1,0:T(8,128)(2,1)}, f32[32,256]{1,0:T(8,128)}) custom-call(f32[3,14]{1,0:T(4,128)} %taps.1, bf16[32,8,16,128]{3,2,1,0:T(8,128)(2,1)} %orbitals_in.1, bf16[32,256]{1,0:T(8,128)(2,1)} %panels_in.1), custom_call_target="tpu_custom_call" | custom-call | tf_op jit(solution)/shard_map/pallas_call | solution.py:441
  74.2 0.0 copy-start
  74.2 2.6 %copy.5 = bf16[32,8,16,128]{3,2,1,0:T(8,128)(2,1)} copy(bf16[32,8,16,128]{3,0,2,1:T(8,128)(2,1)} %bitcast.1) | data formatting | bytes 2097152
  76.8 0.0 copy-done
  76.8 0.6 copy.7
Async XLA Ops:
  74.2 2.6 %copy-start = (f32[32,256]{1,0:T(8,128)S(1)}, f32[32,256]{1,0:T(8,128)}, u32[]{:S(2)}) copy-start(f32[32,256]{1,0:T(8,128)} %get-tuple-element.11) | copy-start | bytes 98308
